TPU v7x, 32 devices: a whole 2x2x4 slice. The times are simulated.
32 devices in a mesh: parts: 2 (over y), gx: 4 (over z), gy: 2 (over x), gz: 2 (over core).
Axes of the slice: x: 2, y: 2, z: 4, core: 2. Of those that a mesh axis runs over, the one named last changes fastest.
Arguments:
- atom_types: int32 [131072], P(('parts', 'gx', 'gy', 'gz')), parts along dimension 0, may hold values from 0 to 3
- potential: float32 [131072], P(('parts', 'gx', 'gy', 'gz')), parts along dimension 0, may hold values from -2 to 2
- guess: float32 [2, 131072], P(None, ('parts', 'gx', 'gy', 'gz')), parts along dimension 1, may hold values from -3 to 3
- type_electroneg: float32 [4], replicated, may hold values from 3 to 7
- type_hardness: float32 [4], replicated, may hold values from 1 to 8
- local_tiles: bfloat16 [2048, 128, 128], P(('parts', 'gx', 'gy', 'gz')), parts along dimension 0, may hold values from -0.00083984375 to 0.00083984375
- local_pairs: int32 [2, 2048], P(None, ('parts', 'gx', 'gy', 'gz')), parts along dimension 1, may hold values from 0 to 31, as said below
- local_count: int32 [32], P(('parts', 'gx', 'gy', 'gz')), parts along dimension 0, may hold values from 32 to 64
- ghost_tiles: bfloat16 [2, 1024, 128, 128], P(None, ('parts', 'gx', 'gy', 'gz')), parts along dimension 1, may hold values from -0.00083984375 to 0.00083984375
- ghost_blocks: int32 [2, 1024], P(None, ('parts', 'gx', 'gy', 'gz')), parts along dimension 1, may hold values from 0 to 31, as said below
- send_rows: int32 [2, 131072], P(None, ('parts', 'gx', 'gy', 'gz')), parts along dimension 1, may hold values from 0 to 4095, as said below
Outputs:
- solution: float32 [2, 131072], P(None, ('parts', 'gx', 'gy', 'gz')), parts along dimension 1
There are 2 independent parts, one for each index of `parts`. A program takes and returns all parts, laid end to end along the dimension named above; an argument that names none is the same for every part. Nothing has to cross between parts.
Inputs may be any that keep to these rules, and one draw needn't show every extreme that they name: In each brick's 64 slots, local_pairs[0] names every block 0 to 31 exactly 2 times, and so does local_pairs[1]. `ghost_blocks`: for each direction and brick, the 32 entries are a permutation of the blocks. `send_rows`: for each direction and brick, the 4096 entries are a permutation of the brick's local atom indices; each aligned block of 128 entries starting at a multiple of 128 holds all atoms of one block of the brick.
All inputs are finite; a program needn't handle non-finite values.
Results may differ from a plain program's by a relative error of at most 0.0003.
Values may be sent and summed in bfloat16 or wider, within the bound.
A program may use at most 64 MiB of HBM per device.

v0:
```python
import jax
import jax.numpy as jnp
from jax import lax
from jax.sharding import PartitionSpec as P

TILE = 128
ITERS = 3


def shifted(block, axis, distance):
    devices = range(lax.axis_size(axis))
    route = [((i - distance) % len(devices), i) for i in devices]
    return lax.ppermute(block, axis, route)


def lookup(atom_ids, table):
    type_codes = jnp.arange(table.shape[0], dtype=jnp.int32)
    return jnp.sum(
        jnp.where(atom_ids[None, :] == type_codes[:, None], table[:, None], jnp.float32(0.0)),
        axis=0,
    )


def halves(vector):
    upper_part = vector.astype(jnp.bfloat16)
    pinned = lax.optimization_barrier(upper_part)
    lower_part = (vector - pinned.astype(jnp.float32)).astype(jnp.bfloat16)
    return (upper_part, lower_part)


def pick_blocks(vector, chosen):
    shaped = vector.reshape(vector.shape[0], -1, TILE)
    onehot = (chosen[:, None] == jnp.arange(shaped.shape[1], dtype=jnp.int32)[None, :]).astype(
        vector.dtype
    )
    picked = jnp.einsum(
        "kb,sbt->skt",
        onehot,
        shaped,
        precision=lax.Precision.HIGHEST,
        preferred_element_type=jnp.float32,
    )
    return picked.astype(vector.dtype)


def spread(values, chosen, blocks):
    onehot = (chosen[:, None] == jnp.arange(blocks, dtype=jnp.int32)[None, :]).astype(jnp.float32)
    summed = jnp.einsum("kb,skt->sbt", onehot, values, precision=lax.Precision.HIGHEST)
    return summed.reshape(values.shape[0], blocks * TILE)


def ghost_maps(send_ids):
    grouped = send_ids.reshape(-1, TILE)
    block_of = grouped[:, 0] // TILE
    within = grouped % TILE
    permuter = (within[:, :, None] == jnp.arange(TILE, dtype=jnp.int32)[None, None, :]).astype(
        jnp.float32
    )
    return (block_of, permuter)


def gather_rows(vector, maps):
    block_of, permuter = maps
    picked = pick_blocks(vector, block_of)
    ordered = jnp.einsum("kic,skc->ski", permuter, picked, precision=lax.Precision.HIGHEST)
    return ordered.reshape(vector.shape[0], -1)


def add_rows(result, values, maps, blocks):
    block_of, permuter = maps
    placed = jnp.einsum(
        "kic,ski->skc",
        permuter,
        values.reshape(values.shape[0], -1, TILE),
        precision=lax.Precision.HIGHEST,
    )
    return result + spread(placed, block_of, blocks)


def forward(tile_set, upper_part, lower_part):
    first = jnp.einsum("krc,skc->skr", tile_set, upper_part, preferred_element_type=jnp.float32)
    return first + jnp.einsum(
        "krc,skc->skr", tile_set, lower_part, preferred_element_type=jnp.float32
    )


def transposed(tile_set, upper_part, lower_part):
    first = jnp.einsum("krc,skr->skc", tile_set, upper_part, preferred_element_type=jnp.float32)
    return first + jnp.einsum(
        "krc,skr->skc", tile_set, lower_part, preferred_element_type=jnp.float32
    )


def inner(left_vec, right_vec):
    return lax.psum(jnp.sum(left_vec * right_vec, axis=1), ("gx", "gy", "gz"))


def shards(
    atom_types,
    potential,
    guess,
    type_electroneg,
    type_hardness,
    local_tiles,
    local_pairs,
    local_count,
    ghost_tiles,
    ghost_blocks,
    send_rows,
):
    electro = lookup(atom_types, type_electroneg)
    hardness = lookup(atom_types, type_hardness)
    target = jnp.stack([-(electro + potential), -jnp.ones_like(potential)])
    blocks = guess.shape[1] // TILE
    living = (jnp.arange(local_tiles.shape[0], dtype=jnp.int32) < local_count[0]).astype(
        jnp.float32
    )[None, :, None]
    own_maps = (ghost_maps(send_rows[0]), ghost_maps(send_rows[1]))

    def operate(vector):
        upper_part, lower_part = halves(vector)
        onward = (
            forward(
                local_tiles,
                pick_blocks(upper_part, local_pairs[1]),
                pick_blocks(lower_part, local_pairs[1]),
            )
            * living
        )
        behind = (
            transposed(
                local_tiles,
                pick_blocks(upper_part, local_pairs[0]),
                pick_blocks(lower_part, local_pairs[0]),
            )
            * living
        )
        result = (
            hardness[None, :] * vector
            + spread(onward, local_pairs[0], blocks)
            + spread(behind, local_pairs[1], blocks)
        )
        for side_index in range(2):
            exported = gather_rows(vector, own_maps[side_index])
            if side_index == 0:
                ghosts = shifted(exported.astype(jnp.bfloat16), "gx", -1).astype(exported.dtype)
            else:
                ghosts = shifted(exported.astype(jnp.bfloat16), ("gy", "gz"), -1).astype(
                    exported.dtype
                )
            ghost_upper, ghost_lower = halves(ghosts)
            onward = forward(
                ghost_tiles[side_index],
                ghost_upper.reshape(2, -1, TILE),
                ghost_lower.reshape(2, -1, TILE),
            )
            result = result + spread(onward, ghost_blocks[side_index], blocks)
            chosen = ghost_blocks[side_index]
            partial_vec = transposed(
                ghost_tiles[side_index],
                pick_blocks(upper_part, chosen),
                pick_blocks(lower_part, chosen),
            ).reshape(2, -1)
            if side_index == 0:
                returned = shifted(partial_vec.astype(jnp.bfloat16), "gx", 1).astype(
                    partial_vec.dtype
                )
            else:
                returned = shifted(partial_vec.astype(jnp.bfloat16), ("gy", "gz"), 1).astype(
                    partial_vec.dtype
                )
            result = add_rows(result, returned, own_maps[side_index], blocks)
        return result

    iterate = guess
    residual = target - operate(guess)
    direction = residual
    norm_now = inner(residual, residual)
    for sweep_index in range(ITERS):
        product_vec = operate(direction)
        step_size = norm_now / inner(direction, product_vec)
        iterate = iterate + step_size[:, None] * direction
        if sweep_index + 1 < ITERS:
            residual = residual - step_size[:, None] * product_vec
            norm_next = inner(residual, residual)
            direction = residual + (norm_next / norm_now)[:, None] * direction
            norm_now = norm_next
    return iterate


def solution(mesh):
    in_specs = (
        P(("parts", "gx", "gy", "gz")),
        P(("parts", "gx", "gy", "gz")),
        P(None, ("parts", "gx", "gy", "gz")),
        P(),
        P(),
        P(("parts", "gx", "gy", "gz"), None, None),
        P(None, ("parts", "gx", "gy", "gz")),
        P(("parts", "gx", "gy", "gz")),
        P(None, ("parts", "gx", "gy", "gz"), None, None),
        P(None, ("parts", "gx", "gy", "gz")),
        P(None, ("parts", "gx", "gy", "gz")),
    )
    out_specs = P(None, ("parts", "gx", "gy", "gz"))
    return jax.shard_map(shards, mesh=mesh, in_specs=in_specs, out_specs=out_specs, check_vma=False)
```

profile of v0, /device:TPU:0, one launch (start us, length us, event | category | flops | bytes accessed | tf_op | source)
XLA Modules:
  0.0 254.5 jit_solution(6550656047433501880)
XLA Ops:
  0.0 1.0 fusion.525
  1.1 1.0 fusion.185
  2.0 2.0 fusion.47
  4.0 5.1 %collective-permute-start = (bf16[2,4096]{1,0:T(2,128)(2,1)S(1)}, bf16[2,4096]{1,0:T(2,128)(2,1)S(1)}, u32[]{:S(2)}, u32[]{:S(2)}) collective-permute-start(bf16[2,4096]{1,0:T(2,128)(2,1)S(1)} %fusion.47), channel_id=1, source_target_pairs={{4,0},{8,4},{12,8},{0,12},{5,1},{9,5},{13,9},{1,13},{6,2},{10,6},{... | collective-permute-start | bytes 49160 | tf_op jit(solution)/shard_map/ppermute | solution.py:13
  9.2 1.1 fusion.183
  10.3 2.0 fusion.55
  12.3 0.7 collective-permute-start.2
  13.0 0.8 convert_element_type.533
  13.8 0.8 convert_bitcast_fusion
  14.6 0.8 slice_bitcast_fusion.1
  15.3 0.8 fusion.253
  16.5 1.6 fusion.112
  18.1 1.6 fusion.31
  21.9 0.6 fusion.527
  22.6 0.7 fusion.166
  24.1 1.2 fusion.526
  25.2 1.2 fusion.167
  27.1 0.6 fusion.116
  27.7 0.7 fusion.114
  28.6 0.9 fusion.14
  29.7 0.9 fusion.6
  30.8 0.6 fusion.88
  31.4 0.7 fusion.86
  34.5 1.2 fusion.529
  35.8 1.2 fusion.528
  37.1 0.7 fusion.531
  37.9 0.6 fusion.530
  38.5 2.0 fusion.49
  40.5 3.8 %collective-permute-start.4 = (bf16[2,4096]{1,0:T(2,128)(2,1)S(1)}, bf16[2,4096]{1,0:T(2,128)(2,1)S(1)}, u32[]{:S(2)}, u32[]{:S(2)}) collective-permute-start(bf16[2,4096]{1,0:T(2,128)(2,1)S(1)} %fusion.49), channel_id=1, source_target_pairs={{4,0},{8,4},{12,8},{0,12},{5,1},{9,5},{13,9},{1,13},{6,2},{10,6},{... | collective-permute-start | bytes 49160 | tf_op jit(solution)/shard_map/ppermute | solution.py:13
  45.4 2.0 fusion.57
  47.4 1.5 collective-permute-start.6
  50.1 0.6 fusion.109
  50.8 0.7 fusion.107
  51.6 0.9 fusion.12
  52.8 0.9 fusion.4
  54.5 0.7 fusion.79
  55.6 34.0 %all-reduce.1 = (f32[2]{0:T(128)S(1)}, f32[2]{0:T(128)S(1)}) all-reduce(f32[2]{0:T(128)S(1)} %get-tuple-element.6, f32[2]{0:T(128)S(1)} %get-tuple-element.5), channel_id=1, replica_groups=mesh['parts'=2,'gx'=4,'gy'=2,'gz'=2] {'gx','gy','gz'}, use_global_device_ids=true, to_apply=%region_3.4 | all-reduce | flops 4 | bytes 32 | tf_op jit(solution)/shard_map/psum | solution.py:95
  89.9 29.5 %psum.44 = f32[2]{0:T(128)S(1)} all-reduce(f32[2]{0:T(128)S(1)} %get-tuple-element.19), channel_id=1, replica_groups=mesh['parts'=2,'gx'=4,'gy'=2,'gz'=2] {'gx','gy','gz'}, use_global_device_ids=true, to_apply=%region_7.8 | all-reduce | flops 2 | bytes 16 | tf_op jit(solution)/shard_map/psum | solution.py:95
  121.6 1.2 fusion.533
  122.9 1.2 fusion.532
  124.2 0.7 fusion.535
  125.0 0.6 fusion.534
  125.6 2.0 fusion.51
  128.5 2.0 collective-permute-start.9
  130.5 2.0 fusion.59
  134.9 0.7 fusion.100
  135.8 0.9 fusion.10
  136.8 0.9 fusion.2
  138.6 0.7 fusion.72
  139.6 32.0 %psum.45 = f32[2]{0:T(128)S(1)} all-reduce(f32[2]{0:T(128)S(1)} %get-tuple-element.15), channel_id=1, replica_groups=mesh['parts'=2,'gx'=4,'gy'=2,'gz'=2] {'gx','gy','gz'}, use_global_device_ids=true, to_apply=%region_9.10 | all-reduce | flops 2 | bytes 16 | tf_op jit(solution)/shard_map/psum | solution.py:95
  171.8 29.7 %psum.46 = f32[2]{0:T(128)S(1)} all-reduce(f32[2]{0:T(128)S(1)} %get-tuple-element.13), channel_id=1, replica_groups=mesh['parts'=2,'gx'=4,'gy'=2,'gz'=2] {'gx','gy','gz'}, use_global_device_ids=true, to_apply=%region_11.12 | all-reduce | flops 2 | bytes 16 | tf_op jit(solution)/shard_map/psum | solution.py:95
  203.8 1.2 fusion.537
  205.1 1.2 fusion.536
  206.4 0.7 fusion.539
  207.2 0.6 fusion.538
  207.8 2.0 fusion.53
  210.6 2.0 collective-permute-start.13
  212.7 2.0 fusion.61
  217.1 0.7 fusion.93
  217.9 0.9 fusion.8
  219.0 0.9 fusion
  220.8 0.7 fusion.65
  221.8 32.0 %psum.47 = f32[2]{0:T(128)S(1)} all-reduce(f32[2]{0:T(128)S(1)} %fusion.169), channel_id=1, replica_groups=mesh['parts'=2,'gx'=4,'gy'=2,'gz'=2] {'gx','gy','gz'}, use_global_device_ids=true, to_apply=%region_13.14 | all-reduce | flops 2 | bytes 16 | tf_op jit(solution)/shard_map/psum | solution.py:95
  253.8 0.7 multiply_add_fusion
  (171 shorter events, 25.6 us)
Async XLA Ops:
  0.0 21.9 %copy-start = (bf16[64,128,128]{2,1,0:T(8,128)(2,1)S(1)}, bf16[64,128,128]{2,1,0:T(8,128)(2,1)}, u32[]{:S(2)}) copy-start(bf16[64,128,128]{2,1,0:T(8,128)(2,1)} %param.16) | copy-start | bytes 6291460
  4.0 23.1 %collective-permute-start = (bf16[2,4096]{1,0:T(2,128)(2,1)S(1)}, bf16[2,4096]{1,0:T(2,128)(2,1)S(1)}, u32[]{:S(2)}, u32[]{:S(2)}) collective-permute-start(bf16[2,4096]{1,0:T(2,128)(2,1)S(1)} %fusion.47), channel_id=1, source_target_pairs={{4,0},{8,4},{12,8},{0,12},{5,1},{9,5},{13,9},{1,13},{6,2},{10,6},{... | collective-permute-start | bytes 49160 | tf_op jit(solution)/shard_map/ppermute | solution.py:13
  9.2 10.9 %copy-start.1 = (bf16[2,32,128,128]{3,2,1,0:T(8,128)(2,1)S(1)}, bf16[2,32,128,128]{3,2,1,0:T(8,128)(2,1)}, u32[]{:S(2)}) copy-start(bf16[2,32,128,128]{3,2,1,0:T(8,128)(2,1)} %param.19) | copy-start | bytes 6291460
  12.3 18.4 %collective-permute-start.2 = (bf16[2,4096]{1,0:T(2,128)(2,1)S(1)}, bf16[2,4096]{1,0:T(2,128)(2,1)S(1)}, u32[]{:S(2)}, u32[]{:S(2)}) collective-permute-start(bf16[2,4096]{1,0:T(2,128)(2,1)S(1)} %fusion.55), channel_id=1, source_target_pairs={{1,0},{2,1},{3,2},{0,3},{5,4},{6,5},{7,6},{4,7},{9,8},{10,9},{11,1... | collective-permute-start | bytes 49160 | tf_op jit(solution)/shard_map/ppermute | solution.py:13
  16.5 4.5 %copy-start.9 = (s32[2,64]{1,0:T(2,128)S(1)}, s32[2,64]{1,0:T(2,128)}, u32[]{:S(2)}) copy-start(s32[2,64]{1,0:T(2,128)} %param.17) | copy-start | bytes 1540
  19.7 8.8 %collective-permute-start.1 = (bf16[2,4096]{1,0:T(2,128)(2,1)S(1)}, bf16[2,4096]{1,0:T(2,128)(2,1)S(1)}, u32[]{:S(2)}, u32[]{:S(2)}) collective-permute-start(bf16[2,4096]{1,0:T(2,128)(2,1)S(1)} %fusion.31), channel_id=1, source_target_pairs={{12,0},{0,4},{4,8},{8,12},{13,1},{1,5},{5,9},{9,13},{14,2},{2,6},{... | collective-permute-start | bytes 49160 | tf_op jit(solution)/shard_map/ppermute | solution.py:13
  20.9 8.7 %collective-permute-start.3 = (bf16[2,4096]{1,0:T(2,128)(2,1)S(1)}, bf16[2,4096]{1,0:T(2,128)(2,1)S(1)}, u32[]{:S(2)}, u32[]{:S(2)}) collective-permute-start(bf16[2,4096]{1,0:T(2,128)(2,1)S(1)} %fusion.33), channel_id=1, source_target_pairs={{3,0},{0,1},{1,2},{2,3},{7,4},{4,5},{5,6},{6,7},{11,8},{8,9},{9,10... | collective-permute-start | bytes 49160 | tf_op jit(solution)/shard_map/ppermute | solution.py:13
  24.0 2.4 copy-start.7
  24.0 2.4 copy-start.10
  24.0 2.4 copy-start.11
  24.0 2.6 %copy-start.8 = (f32[4096]{0:T(1024)S(1)}, f32[4096]{0:T(1024)}, u32[]{:S(2)}) copy-start(f32[4096]{0:T(1024)} %param.12) | copy-start | bytes 49156
  24.1 3.0 %copy-start.2 = (bf16[2,32,128,128]{3,2,1,0:T(8,128)(2,1)S(1)}, bf16[2,32,128,128]{3,2,1,0:T(8,128)(2,1)}, u32[]{:S(2)}) copy-start(bf16[2,32,128,128]{3,2,1,0:T(8,128)(2,1)} %param.19) | copy-start | bytes 6291460
  28.4 3.8 %copy-start.6 = (f32[2,4096]{1,0:T(2,128)S(1)}, f32[2,4096]{1,0:T(2,128)}, u32[]{:S(2)}) copy-start(f32[2,4096]{1,0:T(2,128)} %param.13) | copy-start | bytes 98308
  37.9 6.5 %copy-start.3 = (bf16[2,32,128,128]{3,2,1,0:T(8,128)(2,1)S(1)}, bf16[2,32,128,128]{3,2,1,0:T(8,128)(2,1)}, u32[]{:S(2)}) copy-start(bf16[2,32,128,128]{3,2,1,0:T(8,128)(2,1)} %param.19) | copy-start | bytes 6291460
  40.5 9.6 %collective-permute-start.4 = (bf16[2,4096]{1,0:T(2,128)(2,1)S(1)}, bf16[2,4096]{1,0:T(2,128)(2,1)S(1)}, u32[]{:S(2)}, u32[]{:S(2)}) collective-permute-start(bf16[2,4096]{1,0:T(2,128)(2,1)S(1)} %fusion.49), channel_id=1, source_target_pairs={{4,0},{8,4},{12,8},{0,12},{5,1},{9,5},{13,9},{1,13},{6,2},{10,6},{... | collective-permute-start | bytes 49160 | tf_op jit(solution)/shard_map/ppermute | solution.py:13
  45.1 6.4 %collective-permute-start.5 = (bf16[2,4096]{1,0:T(2,128)(2,1)S(1)}, bf16[2,4096]{1,0:T(2,128)(2,1)S(1)}, u32[]{:S(2)}, u32[]{:S(2)}) collective-permute-start(bf16[2,4096]{1,0:T(2,128)(2,1)S(1)} %fusion.35), channel_id=1, source_target_pairs={{12,0},{0,4},{4,8},{8,12},{13,1},{1,5},{5,9},{9,13},{14,2},{2,6},{... | collective-permute-start | bytes 49160 | tf_op jit(solution)/shard_map/ppermute | solution.py:13
  47.4 6.5 %collective-permute-start.6 = (bf16[2,4096]{1,0:T(2,128)(2,1)S(1)}, bf16[2,4096]{1,0:T(2,128)(2,1)S(1)}, u32[]{:S(2)}, u32[]{:S(2)}) collective-permute-start(bf16[2,4096]{1,0:T(2,128)(2,1)S(1)} %fusion.57), channel_id=1, source_target_pairs={{1,0},{2,1},{3,2},{0,3},{5,4},{6,5},{7,6},{4,7},{9,8},{10,9},{11,1... | collective-permute-start | bytes 49160 | tf_op jit(solution)/shard_map/ppermute | solution.py:13
  49.6 3.2 %collective-permute-start.7 = (bf16[2,4096]{1,0:T(2,128)(2,1)S(1)}, bf16[2,4096]{1,0:T(2,128)(2,1)S(1)}, u32[]{:S(2)}, u32[]{:S(2)}) collective-permute-start(bf16[2,4096]{1,0:T(2,128)(2,1)S(1)} %fusion.37), channel_id=1, source_target_pairs={{3,0},{0,1},{1,2},{2,3},{7,4},{4,5},{5,6},{6,7},{11,8},{8,9},{9,10... | collective-permute-start | bytes 49160 | tf_op jit(solution)/shard_map/ppermute | solution.py:13
  125.0 2.7 %copy-start.4 = (bf16[2,32,128,128]{3,2,1,0:T(8,128)(2,1)S(1)}, bf16[2,32,128,128]{3,2,1,0:T(8,128)(2,1)}, u32[]{:S(2)}) copy-start(bf16[2,32,128,128]{3,2,1,0:T(8,128)(2,1)} %param.19) | copy-start | bytes 6291460
  127.6 6.6 %collective-permute-start.8 = (bf16[2,4096]{1,0:T(2,128)(2,1)S(1)}, bf16[2,4096]{1,0:T(2,128)(2,1)S(1)}, u32[]{:S(2)}, u32[]{:S(2)}) collective-permute-start(bf16[2,4096]{1,0:T(2,128)(2,1)S(1)} %fusion.51), channel_id=1, source_target_pairs={{4,0},{8,4},{12,8},{0,12},{5,1},{9,5},{13,9},{1,13},{6,2},{10,6},{... | collective-permute-start | bytes 49160 | tf_op jit(solution)/shard_map/ppermute | solution.py:13
  128.5 7.3 %collective-permute-start.9 = (bf16[2,4096]{1,0:T(2,128)(2,1)S(1)}, bf16[2,4096]{1,0:T(2,128)(2,1)S(1)}, u32[]{:S(2)}, u32[]{:S(2)}) collective-permute-start(bf16[2,4096]{1,0:T(2,128)(2,1)S(1)} %fusion.39), channel_id=1, source_target_pairs={{12,0},{0,4},{4,8},{8,12},{13,1},{1,5},{5,9},{9,13},{14,2},{2,6},{... | collective-permute-start | bytes 49160 | tf_op jit(solution)/shard_map/ppermute | solution.py:13
  132.5 5.4 %collective-permute-start.10 = (bf16[2,4096]{1,0:T(2,128)(2,1)S(1)}, bf16[2,4096]{1,0:T(2,128)(2,1)S(1)}, u32[]{:S(2)}, u32[]{:S(2)}) collective-permute-start(bf16[2,4096]{1,0:T(2,128)(2,1)S(1)} %fusion.59), channel_id=1, source_target_pairs={{1,0},{2,1},{3,2},{0,3},{5,4},{6,5},{7,6},{4,7},{9,8},{10,9},{11,1... | collective-permute-start | bytes 49160 | tf_op jit(solution)/shard_map/ppermute | solution.py:13
  133.3 3.5 %collective-permute-start.11 = (bf16[2,4096]{1,0:T(2,128)(2,1)S(1)}, bf16[2,4096]{1,0:T(2,128)(2,1)S(1)}, u32[]{:S(2)}, u32[]{:S(2)}) collective-permute-start(bf16[2,4096]{1,0:T(2,128)(2,1)S(1)} %fusion.41), channel_id=1, source_target_pairs={{3,0},{0,1},{1,2},{2,3},{7,4},{4,5},{5,6},{6,7},{11,8},{8,9},{9,10... | collective-permute-start | bytes 49160 | tf_op jit(solution)/shard_map/ppermute | solution.py:13
  207.2 2.7 %copy-start.5 = (bf16[2,32,128,128]{3,2,1,0:T(8,128)(2,1)S(1)}, bf16[2,32,128,128]{3,2,1,0:T(8,128)(2,1)}, u32[]{:S(2)}) copy-start(bf16[2,32,128,128]{3,2,1,0:T(8,128)(2,1)} %param.19) | copy-start | bytes 6291460
  209.8 6.7 %collective-permute-start.12 = (bf16[2,4096]{1,0:T(2,128)(2,1)S(1)}, bf16[2,4096]{1,0:T(2,128)(2,1)S(1)}, u32[]{:S(2)}, u32[]{:S(2)}) collective-permute-start(bf16[2,4096]{1,0:T(2,128)(2,1)S(1)} %fusion.53), channel_id=1, source_target_pairs={{4,0},{8,4},{12,8},{0,12},{5,1},{9,5},{13,9},{1,13},{6,2},{10,6},{... | collective-permute-start | bytes 49160 | tf_op jit(solution)/shard_map/ppermute | solution.py:13
  210.6 7.3 %collective-permute-start.13 = (bf16[2,4096]{1,0:T(2,128)(2,1)S(1)}, bf16[2,4096]{1,0:T(2,128)(2,1)S(1)}, u32[]{:S(2)}, u32[]{:S(2)}) collective-permute-start(bf16[2,4096]{1,0:T(2,128)(2,1)S(1)} %fusion.43), channel_id=1, source_target_pairs={{12,0},{0,4},{4,8},{8,12},{13,1},{1,5},{5,9},{9,13},{14,2},{2,6},{... | collective-permute-start | bytes 49160 | tf_op jit(solution)/shard_map/ppermute | solution.py:13
  214.7 5.4 %collective-permute-start.14 = (bf16[2,4096]{1,0:T(2,128)(2,1)S(1)}, bf16[2,4096]{1,0:T(2,128)(2,1)S(1)}, u32[]{:S(2)}, u32[]{:S(2)}) collective-permute-start(bf16[2,4096]{1,0:T(2,128)(2,1)S(1)} %fusion.61), channel_id=1, source_target_pairs={{1,0},{2,1},{3,2},{0,3},{5,4},{6,5},{7,6},{4,7},{9,8},{10,9},{11,1... | collective-permute-start | bytes 49160 | tf_op jit(solution)/shard_map/ppermute | solution.py:13
  215.5 3.5 %collective-permute-start.15 = (bf16[2,4096]{1,0:T(2,128)(2,1)S(1)}, bf16[2,4096]{1,0:T(2,128)(2,1)S(1)}, u32[]{:S(2)}, u32[]{:S(2)}) collective-permute-start(bf16[2,4096]{1,0:T(2,128)(2,1)S(1)} %fusion.45), channel_id=1, source_target_pairs={{3,0},{0,1},{1,2},{2,3},{7,4},{4,5},{5,6},{6,7},{11,8},{8,9},{9,10... | collective-permute-start | bytes 49160 | tf_op jit(solution)/shard_map/ppermute | solution.py:13
where the time goes:
time: 255 us
  blocking collectives  157 us (62%)
  matrix products  70.6 us (28%)
  starting transfers between devices  16.7 us (7%)
  other arithmetic  4.88 us (2%)
  local copies, waits for them, and re-layouts  3.49 us (1%)
    psum x5, blocking collectives, inner(): return lax.psum(jnp.sum(left_vec * right_vec, axis=1), ('gx', 'gy', 'gz'))  157 us
    ppermute x16, starting transfers between devices, shifted(): return lax.ppermute(block, axis, route)  16.7 us
    dot_general x8, matrix products, gather_rows(): jnp.einsum('kic,skc->ski', permuter, picked, precision=lax.Precision.HIGH...  15.9 us
    dot_general x12, matrix products, forward(): jnp.einsum('krc,skc->skr', tile_set, lower_part, preferred_element_type=j...  9.92 us
    dot_general x12, matrix products, forward(): jnp.einsum('krc,skc->skr', tile_set, upper_part, preferred_element_type=j...  9.8 us
    dot_general x40, matrix products, pick_blocks(): jnp.einsum('kb,sbt->skt', onehot, shaped, precision=lax.Precision.HIGHEST...  9.56 us
    dot_general x8, matrix products, add_rows(): jnp.einsum('kic,ski->skc', permuter, values.reshape(values.shape[0], -1,...  7.34 us
    dot_general x12, matrix products, transposed(): jnp.einsum('krc,skr->skc', tile_set, lower_part, preferred_element_type=j...  6.94 us
  transfers between devices with their start and end apart: 16, of which 1 were waited for; matrix products, arithmetic and copies ran while one was open for 17% of the time, Pallas kernels for 0%

commit v1 on v0

v1 whole, which is shorter than its diff:
```python
import functools

import jax
import jax.numpy as jnp
from jax import lax
from jax.experimental import pallas as pl
from jax.experimental.pallas import tpu as pltpu
from jax.sharding import PartitionSpec as P

TILE = 128
ITERS = 3
DIRECT = 16
MESH = pl.DeviceIdType.MESH
F32 = jnp.float32
I32 = jnp.int32
NT = (((1,), (1,)), ((), ()))
NN = (((1,), (0,)), ((), ()))


def dot(lhs, rhs, dims):
    return lax.dot_general(lhs, rhs, dims, preferred_element_type=F32)


def places(sizes):
    n_gx, n_gy, n_gz = sizes
    across = n_gy * n_gz
    u = lax.axis_index("gx")
    v = lax.axis_index("gy") * n_gz + lax.axis_index("gz")

    def brick(u_at, v_at):
        return {"gx": u_at, "gy": v_at // n_gz, "gz": lax.rem(v_at, n_gz)}

    def shift(at, by, size):
        return lax.rem(at + by, size)

    ahead = (brick(shift(u, 1, n_gx), v), brick(u, shift(v, 1, across)))
    back = (brick(shift(u, n_gx - 1, n_gx), v), brick(u, shift(v, across - 1, across)))
    whole = n_gx * across
    if whole <= DIRECT:
        me = u * across + v

        def peer(step):
            at = lax.rem(me + step, whole)
            return brick(at // across, lax.rem(at, across))

        stages = [(whole, me, peer)]
    else:
        stages = [
            (n_gx, u, lambda step: brick(shift(u, step, n_gx), v)),
            (across, v, lambda step: brick(u, shift(v, step, across))),
        ]
    return ahead, back, stages


def kernel(
    sizes,
    types_ref,
    potential_ref,
    guess_ref,
    electro_ref,
    hard_ref,
    local_hbm,
    pairs_ref,
    count_ref,
    ghost_hbm,
    gblocks_ref,
    gblocks_s,
    send_ref,
    out_ref,
    lt,
    gt,
    gp,
    rows,
    rows_in,
    table_v,
    table_s,
    own_v,
    own_s,
    next_v,
    next_s,
    vec,
    vec_in,
    part,
    part_in,
    lh,
    gl,
    hd,
    xs,
    rs,
    ps,
    red,
    load_sem,
    rows_sem,
    vec_sem,
    part_sem,
    red_sem,
):
    blocks = types_ref.shape[0]
    ahead, back, stages = places(sizes)

    barrier = pltpu.get_barrier_semaphore()
    greeted = 0
    for size, _, peer in stages:
        greeted += size - 1
        for step in range(1, size):
            pl.semaphore_signal(barrier, inc=1, device_id=peer(step), device_id_type=MESH)

    load_local = pltpu.make_async_copy(local_hbm, lt, load_sem.at[0])
    load_local.start()
    load_ghost = pltpu.make_async_copy(ghost_hbm, gt, load_sem.at[1])
    load_ghost.start()

    for b in range(blocks):
        cut = slice(b * TILE, (b + 1) * TILE)
        piece = send_ref[:, cut]
        rows[0, b : b + 1, :] = piece[0:1]
        rows[1, b : b + 1, :] = piece[1:2]
        begin = guess_ref[:, cut]
        vec[0, b] = begin
        xs[b] = begin

    slots = pairs_ref.shape[1]
    slot = lax.broadcasted_iota(I32, (blocks, slots), 1)
    block = lax.broadcasted_iota(I32, (blocks, slots), 0)
    live = slot < count_ref[0]
    pair_row = jnp.broadcast_to(pairs_ref[0:1, :], (blocks, slots))
    pair_col = jnp.broadcast_to(pairs_ref[1:2, :], (blocks, slots))
    columns = []
    partners = []
    for mine, other in ((pair_row, pair_col), (pair_col, pair_row)):
        hit = mine == block
        first = jnp.min(jnp.where(hit, slot, slots - 1), axis=1, keepdims=True)
        last = jnp.max(jnp.where(hit, slot, 0), axis=1, keepdims=True)
        for found in (first, last):
            columns.append(found)
            value = jnp.where(live, other, blocks)
            partners.append(
                jnp.max(jnp.where(slot == found, value, 0), axis=1, keepdims=True)
            )
    columns = columns + partners
    slot_g = lax.broadcasted_iota(I32, (blocks, blocks), 1)
    block_g = lax.broadcasted_iota(I32, (blocks, blocks), 0)
    for d in range(2):
        named = jnp.broadcast_to(gblocks_ref[d : d + 1, :], (blocks, blocks))
        columns.append(jnp.max(jnp.where(named == block_g, slot_g, 0), axis=1, keepdims=True))
    lane = lax.broadcasted_iota(I32, (blocks, TILE), 1)
    table = jnp.zeros((blocks, TILE), I32)
    for q, column in enumerate(columns):
        table = jnp.where(lane == q, column, table)
    table_v[...] = table
    load_table = pltpu.make_async_copy(table_v, table_s, load_sem.at[2])
    load_table.start()
    own_v[...] = jnp.zeros(own_v.shape, I32)
    slot_k = lax.broadcasted_iota(I32, (blocks, TILE), 0)
    for d in range(2):
        at = jnp.broadcast_to(rows[d][:, 0:1] // TILE, (blocks, TILE))
        own_v[d : d + 1, :] = jnp.max(
            jnp.where(at == lane, slot_k, 0), axis=0, keepdims=True
        )
    load_own = pltpu.make_async_copy(own_v, own_s, load_sem.at[3])
    load_own.start()

    pl.semaphore_wait(barrier, greeted)

    rows_copy = []
    for d in range(2):
        copy = pltpu.make_async_remote_copy(
            src_ref=rows.at[d],
            dst_ref=rows_in.at[d],
            send_sem=rows_sem.at[0, d],
            recv_sem=rows_sem.at[1, d],
            device_id=back[d],
            device_id_type=MESH,
        )
        copy.start()
        rows_copy.append(copy)

    def send(buffer, landing, sems, apply, d, target):
        copy = pltpu.make_async_remote_copy(
            src_ref=buffer,
            dst_ref=landing,
            send_sem=sems.at[0, apply, d],
            recv_sem=sems.at[1, apply, d],
            device_id=target,
            device_id_type=MESH,
        )
        copy.start()
        return copy

    types = types_ref[...]
    hard = jnp.zeros(types.shape, F32)
    electro = jnp.zeros(types.shape, F32)
    for code in range(hard_ref.shape[0]):
        hard = jnp.where(types == code, hard_ref[code], hard)
        electro = jnp.where(types == code, electro_ref[code], electro)
    wanted = -(electro + potential_ref[...])
    system = lax.broadcasted_iota(I32, (2, TILE), 0)
    for b in range(blocks):
        hd[b] = jnp.broadcast_to(hard[b : b + 1], (2, TILE))
        rs[b] = jnp.where(system == 0, jnp.broadcast_to(wanted[b : b + 1], (2, TILE)), -1.0)

    lh[blocks] = jnp.zeros((8, TILE), F32)
    top = lax.broadcasted_iota(I32, (8, TILE), 0) < 4

    def split(vector):
        upper = vector.astype(jnp.bfloat16).astype(F32)
        return jnp.concatenate([upper, vector - upper] * 2, axis=1)

    def join(one, two):
        return jnp.where(top, one, two).astype(jnp.bfloat16)

    def parts_of(both):
        one = both[0:2, :TILE] + both[2:4, :TILE]
        two = both[4:6, TILE:] + both[6:8, TILE:]
        return one, two

    def square(a, b, c, d):
        return jnp.concatenate(
            [jnp.concatenate([a, b], axis=1), jnp.concatenate([c, d], axis=1)], axis=0
        )

    def looped(steps, unroll, body):
        def run(outer, carry):
            for inner in range(unroll):
                body(outer * unroll + inner)
            return carry

        lax.fori_loop(0, steps // unroll, run, 0)

    def local_part(apply):
        def body(pair):
            one = pair * 2
            two = one + 1
            s = [(table_s[one, q], table_s[two, q]) for q in range(8)]
            left = jnp.concatenate(
                [join(lh[s[4][0]], lh[s[4][1]]), join(lh[s[5][0]], lh[s[5][1]])], axis=1
            )
            onward = dot(
                left, square(lt[s[0][0]], lt[s[1][0]], lt[s[0][1]], lt[s[1][1]]), NT
            )
            left = jnp.concatenate(
                [join(lh[s[6][0]], lh[s[6][1]]), join(lh[s[7][0]], lh[s[7][1]])], axis=1
            )
            behind = dot(
                left, square(lt[s[2][0]], lt[s[2][1]], lt[s[3][0]], lt[s[3][1]]), NN
            )
            sum_one, sum_two = parts_of(onward + behind)
            ps[one] = hd[one] * vec[apply, one] + sum_one
            ps[two] = hd[two] * vec[apply, two] + sum_two

        looped(blocks // 2, 4, body)

    def partials(apply):
        def body(k):
            left = join(lh[gblocks_s[0, k]], lh[gblocks_s[1, k]])
            both = dot(left, jnp.concatenate([gp[0, k], gp[1, k]], axis=1), NN)
            zero, first = parts_of(both)
            part[apply, 0, k] = zero
            part[apply, 1, k] = first

        looped(blocks, 8, body)

    def ghost_part():
        def body(pair):
            one = pair * 2
            two = one + 1
            k0 = (table_s[one, 8], table_s[two, 8])
            k1 = (table_s[one, 9], table_s[two, 9])
            left = jnp.concatenate(
                [
                    join(gl[0, next_s[k0[0], 0]], gl[0, next_s[k0[1], 0]]),
                    join(gl[1, next_s[k1[0], 1]], gl[1, next_s[k1[1], 1]]),
                ],
                axis=1,
            )
            sum_one, sum_two = parts_of(
                dot(left, square(gp[0, k0[0]], gp[1, k1[0]], gp[0, k0[1]], gp[1, k1[1]]), NT)
            )
            ps[one] = ps[one] + sum_one
            ps[two] = ps[two] + sum_two

        looped(blocks // 2, 4, body)

    def returned(apply):
        def body(b):
            ps[b] = ps[b] + (part_in[apply][0][own_s[0, b]] + part_in[apply][1][own_s[1, b]])

        looped(blocks, 8, body)

    def reorder():
        within_at = lax.broadcasted_iota(I32, (TILE, TILE), 0)

        for d in range(2):

            def body(k):
                within = rows_in[d, pl.ds(k, 1), :]
                within = within - (within // TILE) * TILE
                chosen = jnp.where(within == within_at, 1.0, 0.0).astype(jnp.bfloat16)
                gp[d, k] = dot(gt[d, k], chosen, NT).astype(jnp.bfloat16)

            looped(blocks, 4, body)

    pending = []
    for apply in range(ITERS + 1):
        incoming = []
        for d in range(2):
            incoming.append(
                send(vec.at[apply], vec_in.at[apply, d], vec_sem, apply, d, back[d])
            )
        lh[0:blocks] = split(vec[apply])
        if apply == 0:
            load_local.wait()
            load_table.wait()
            local_part(apply)
            load_ghost.wait()
            for copy in rows_copy:
                copy.wait()
            columns = jnp.zeros((blocks, TILE), I32)
            for d in range(2):
                columns = jnp.where(lane == d, rows_in[d][:, 0:1] // TILE, columns)
            next_v[...] = columns
            load_next = pltpu.make_async_copy(next_v, next_s, load_sem.at[4])
            load_next.start()
            reorder()
            load_next.wait()
            load_own.wait()
        partials(apply)
        back_copies = []
        for d in range(2):
            back_copies.append(
                send(part.at[apply, d], part_in[apply][d], part_sem, apply, d, ahead[d])
            )
        if apply > 0:
            local_part(apply)
        for d in range(2):
            incoming[d].wait()
            gl[d] = split(vec_in[apply, d])
        ghost_part()
        for copy in back_copies:
            copy.wait()
        returned(apply)
        product = ps[...]
        if apply == 0:
            residual = rs[...] - product
            rs[...] = residual
            vec[1] = residual
            continue

        residual = rs[...]
        direction = vec[apply]
        sums = jnp.concatenate(
            [
                jnp.sum(a * b, axis=0)
                for a, b in (
                    (residual, residual),
                    (direction, product),
                    (residual, product),
                    (product, product),
                )
            ],
            axis=0,
        )
        offset = 0
        sem_at = 0
        for size, me, peer in stages:
            mine = offset + me
            red[apply - 1, mine] = sums
            copies = []
            for step in range(1, size):
                copy = pltpu.make_async_remote_copy(
                    src_ref=red.at[apply - 1, mine],
                    dst_ref=red.at[apply - 1, mine],
                    send_sem=red_sem.at[0, apply - 1, sem_at],
                    recv_sem=red_sem.at[1, apply - 1, sem_at],
                    device_id=peer(step),
                    device_id_type=MESH,
                )
                copy.start()
                copies.append(copy)
                sem_at += 1
            for copy in copies:
                copy.wait()
            sums = jnp.sum(red[apply - 1, offset : offset + size], axis=0)
            offset += size
        totals = jnp.broadcast_to(jnp.sum(sums, axis=1, keepdims=True), (8, TILE))
        norm_now = totals[0:2]
        step_size = norm_now / totals[2:4]
        found = xs[...] + step_size[None] * direction
        if apply == ITERS:
            xs[...] = found
        else:
            xs[...] = found
            ratio = jnp.maximum(
                (norm_now + step_size * (step_size * totals[6:8] - 2.0 * totals[4:6])) / norm_now,
                0.0,
            )
            residual = residual - step_size[None] * product
            rs[...] = residual
            vec[apply + 1] = residual + ratio[None] * direction

    for b in range(blocks):
        out_ref[:, b * TILE : (b + 1) * TILE] = xs[b]


def shards(
    sizes,
    atom_types,
    potential,
    guess,
    type_electroneg,
    type_hardness,
    local_tiles,
    local_pairs,
    local_count,
    ghost_tiles,
    ghost_blocks,
    send_rows,
):
    blocks = guess.shape[1] // TILE
    slots = local_tiles.shape[0]
    n_gx, n_gy, n_gz = sizes
    if n_gx * n_gy * n_gz <= DIRECT:
        places_held, peers = n_gx * n_gy * n_gz, n_gx * n_gy * n_gz - 1
    else:
        places_held, peers = n_gx + n_gy * n_gz, n_gx + n_gy * n_gz - 2
    vmem = pl.BlockSpec(memory_space=pltpu.VMEM)
    smem = pl.BlockSpec(memory_space=pltpu.SMEM)
    hbm = pl.BlockSpec(memory_space=pl.ANY)
    applies = ITERS + 1
    vector = (blocks, 2, TILE)
    dma = pltpu.SemaphoreType.DMA
    call = pl.pallas_call(
        functools.partial(kernel, sizes),
        out_shape=jax.ShapeDtypeStruct(guess.shape, F32),
        in_specs=[vmem, vmem, vmem, smem, smem, hbm, vmem, smem, hbm, vmem, smem, vmem],
        out_specs=vmem,
        scratch_shapes=[
            pltpu.VMEM((slots, TILE, TILE), jnp.bfloat16),
            pltpu.VMEM((2, blocks, TILE, TILE), jnp.bfloat16),
            pltpu.VMEM((2, blocks, TILE, TILE), jnp.bfloat16),
            pltpu.VMEM((2, blocks, TILE), I32),
            pltpu.VMEM((2, blocks, TILE), I32),
            pltpu.VMEM((blocks, TILE), I32),
            pltpu.SMEM((blocks, TILE), I32),
            pltpu.VMEM((8, TILE), I32),
            pltpu.SMEM((8, TILE), I32),
            pltpu.VMEM((blocks, TILE), I32),
            pltpu.SMEM((blocks, TILE), I32),
            pltpu.VMEM((applies,) + vector, F32),
            pltpu.VMEM((applies, 2) + vector, F32),
            pltpu.VMEM((applies, 2) + vector, F32),
            [[pltpu.VMEM(vector, F32)] * 2 for _ in range(applies)],
            pltpu.VMEM((blocks + 1, 8, TILE), F32),
            pltpu.VMEM((2, blocks, 8, TILE), F32),
            pltpu.VMEM(vector, F32),
            pltpu.VMEM(vector, F32),
            pltpu.VMEM(vector, F32),
            pltpu.VMEM(vector, F32),
            pltpu.VMEM((ITERS, places_held, 8, TILE), F32),
            dma((5,)),
            dma((2, 2)),
            dma((2, applies, 2)),
            dma((2, applies, 2)),
            dma((2, ITERS, peers)),
        ],
        compiler_params=pltpu.CompilerParams(
            collective_id=0, has_side_effects=True, vmem_limit_bytes=40 * 1024 * 1024
        ),
        name="charges",
    )
    return call(
        atom_types.reshape(blocks, TILE),
        potential.reshape(blocks, TILE),
        guess,
        type_electroneg,
        type_hardness,
        local_tiles,
        local_pairs,
        local_count,
        ghost_tiles,
        ghost_blocks,
        ghost_blocks,
        send_rows,
    )


def solution(mesh):
    everywhere = ("parts", "gx", "gy", "gz")
    in_specs = (
        P(everywhere),
        P(everywhere),
        P(None, everywhere),
        P(),
        P(),
        P(everywhere, None, None),
        P(None, everywhere),
        P(everywhere),
        P(None, everywhere, None, None),
        P(None, everywhere),
        P(None, everywhere),
    )
    sizes = tuple(mesh.shape[name] for name in ("gx", "gy", "gz"))
    return jax.shard_map(
        functools.partial(shards, sizes),
        mesh=mesh,
        in_specs=in_specs,
        out_specs=P(None, everywhere),
        check_vma=False,
    )
```

time: 255 us -> 58.1 us (0.23)
  blocking collectives: 157 us -> 0 us
  matrix products: 70.6 us -> 0 us
  Pallas kernels: 0 us -> 47.5 us
  starting transfers between devices: 16.7 us -> 0 us
  local copies, waits for them, and re-layouts: 3.49 us -> 9.41 us
  other arithmetic: 4.88 us -> 0 us
    psum x5 -> x0, blocking collectives: 157 us -> none  [inner(): return lax.psum(jnp.sum(left_vec * right_vec, axis=1), ('gx', 'gy', 'gz'))]
    dot_general x128 -> x0, matrix products: 70.6 us -> none  [the longest x8 15.9 us: gather_rows(): jnp.einsum('kic,skc->ski', permuter, picked, precision=lax.Precision.HIGH...]
    pallas_call x0 -> x1, Pallas kernels: none -> 47.5 us  [shards(): call(atom_types.reshape(blocks, TILE), potential.reshape(blocks, TILE), g...]
    ppermute x16 -> x0, starting transfers between devices: 16.7 us -> none  [shifted(): return lax.ppermute(block, axis, route)]
    unnamed x26 -> x21, local copies, waits for them, and re-layouts: 0.22 us -> 9.41 us
  transfers between devices with their start and end apart: 16 -> 0, of which waited for: 1 -> 0; matrix products, arithmetic and copies ran while one was open for 17% -> 0% of each run, Pallas kernels for 0% -> 0%
where the time goes in v1:
time: 58.1 us; the launch traced here: 57.6 us
  Pallas kernels  47.5 us (82%)
  local copies, waits for them, and re-layouts  9.41 us (16%)
  between operations  0.68 us (1%)
    pallas_call x1, Pallas kernels, shards(): call(atom_types.reshape(blocks, TILE), potential.reshape(blocks, TILE), g...  47.5 us
    unnamed x21, local copies, waits for them, and re-layouts  9.41 us

profile of v1, /device:TPU:0, one launch (start us, length us, event | category | flops | bytes accessed | tf_op | source)
XLA Modules:
  0.0 57.6 jit_solution(4519101594633221340)
XLA Ops:
  0.7 0.0 copy-start
  0.7 1.6 %copy-done = bf16[64,128,128]{2,1,0:T(8,128)(2,1)S(1)} copy-done((bf16[64,128,128]{2,1,0:T(8,128)(2,1)S(1)}, bf16[64,128,128]{2,1,0:T(8,128)(2,1)}, u32[]{:S(2)}) %copy-start) | copy-done | bytes 2097176
  2.2 0.0 copy-start.1
  2.2 1.6 %copy-done.1 = bf16[2,32,128,128]{3,2,1,0:T(8,128)(2,1)S(1)} copy-done((bf16[2,32,128,128]{3,2,1,0:T(8,128)(2,1)S(1)}, bf16[2,32,128,128]{3,2,1,0:T(8,128)(2,1)}, u32[]{:S(2)}) %copy-start.1) | copy-done | bytes 2097176
  3.8 0.0 copy-start.2
  3.8 0.8 %copy-done.2 = f32[2,4096]{1,0:T(2,128)S(1)} copy-done((f32[2,4096]{1,0:T(2,128)S(1)}, f32[2,4096]{1,0:T(2,128)}, u32[]{:S(2)}) %copy-start.2) | copy-done | bytes 32792
  4.6 0.0 copy-start.3
  4.6 0.8 %copy-done.3 = s32[2,4096]{1,0:T(2,128)S(1)} copy-done((s32[2,4096]{1,0:T(2,128)S(1)}, s32[2,4096]{1,0:T(2,128)}, u32[]{:S(2)}) %copy-start.3) | copy-done | bytes 32792
  5.4 0.0 copy-start.4
  5.4 0.7 %copy-done.4 = s32[4096]{0:T(1024)S(1)} copy-done((s32[4096]{0:T(1024)S(1)}, s32[4096]{0:T(1024)}, u32[]{:S(2)}) %copy-start.4) | copy-done | bytes 16408
  6.1 0.0 copy-start.5
  6.1 0.7 %copy-done.5 = f32[4096]{0:T(1024)S(1)} copy-done((f32[4096]{0:T(1024)S(1)}, f32[4096]{0:T(1024)}, u32[]{:S(2)}) %copy-start.5) | copy-done | bytes 16408
  6.8 0.0 copy-start.6
  6.8 0.7 %copy-done.6 = s32[2,32]{1,0:T(2,128)S(1)} copy-done((s32[2,32]{1,0:T(2,128)S(1)}, s32[2,32]{1,0:T(2,128)}, u32[]{:S(2)}) %copy-start.6) | copy-done | bytes 280
  7.5 0.0 copy-start.7
  7.5 0.7 %copy-done.7 = s32[2,64]{1,0:T(2,128)S(1)} copy-done((s32[2,64]{1,0:T(2,128)S(1)}, s32[2,64]{1,0:T(2,128)}, u32[]{:S(2)}) %copy-start.7) | copy-done | bytes 536
  8.1 0.0 copy-start.8
  8.1 0.7 %copy-done.8 = f32[4]{0:T(128)S(1)} copy-done((f32[4]{0:T(128)S(1)}, f32[4]{0:T(128)}, u32[]{:S(2)}) %copy-start.8) | copy-done | bytes 40
  8.8 0.0 copy-start.9
  8.8 0.7 %copy-done.9 = f32[4]{0:T(128)S(1)} copy-done((f32[4]{0:T(128)S(1)}, f32[4]{0:T(128)}, u32[]{:S(2)}) %copy-start.9) | copy-done | bytes 40
  9.5 47.5 %charges.1 = f32[2,4096]{1,0:T(2,128)S(1)} custom-call(s32[32,128]{1,0:T(8,128)S(1)} %bitcast.2, f32[32,128]{1,0:T(8,128)S(1)} %bitcast.3, f32[2,4096]{1,0:T(2,128)S(1)} %copy-done.2, f32[4]{0:T(128)S(1)} %copy-done.8, f32[4]{0:T(128)S(1)} %copy-done.9, bf16[64,128,128]{2,1,0:T(8,128)(2,1)S(1)} %copy-done, s32[2,64]{1,0:T(2,128)S(1)} %copy-done.7, ...), custom_call_target="tpu_custom_call" | custom-call | tf_op jit(solution)/shard_map/charges/pallas_call | solution.py:471
  57.0 0.6 %copy.14 = f32[2,4096]{1,0:T(2,128)} copy(f32[2,4096]{1,0:T(2,128)S(1)} %charges.1) | data formatting | bytes 65536
Async XLA Ops:
  0.7 1.6 %copy-start = (bf16[64,128,128]{2,1,0:T(8,128)(2,1)S(1)}, bf16[64,128,128]{2,1,0:T(8,128)(2,1)}, u32[]{:S(2)}) copy-start(bf16[64,128,128]{2,1,0:T(8,128)(2,1)} %local_hbm.1) | copy-start | bytes 6291460
  2.2 1.6 %copy-start.1 = (bf16[2,32,128,128]{3,2,1,0:T(8,128)(2,1)S(1)}, bf16[2,32,128,128]{3,2,1,0:T(8,128)(2,1)}, u32[]{:S(2)}) copy-start(bf16[2,32,128,128]{3,2,1,0:T(8,128)(2,1)} %ghost_hbm.1) | copy-start | bytes 6291460
  3.8 0.8 %copy-start.2 = (f32[2,4096]{1,0:T(2,128)S(1)}, f32[2,4096]{1,0:T(2,128)}, u32[]{:S(2)}) copy-start(f32[2,4096]{1,0:T(2,128)} %guess_ref.1) | copy-start | bytes 98308
  4.6 0.8 %copy-start.3 = (s32[2,4096]{1,0:T(2,128)S(1)}, s32[2,4096]{1,0:T(2,128)}, u32[]{:S(2)}) copy-start(s32[2,4096]{1,0:T(2,128)} %send_ref.1) | copy-start | bytes 98308
  5.4 0.7 %copy-start.4 = (s32[4096]{0:T(1024)S(1)}, s32[4096]{0:T(1024)}, u32[]{:S(2)}) copy-start(s32[4096]{0:T(1024)} %param.11) | copy-start | bytes 49156
  6.1 0.7 %copy-start.5 = (f32[4096]{0:T(1024)S(1)}, f32[4096]{0:T(1024)}, u32[]{:S(2)}) copy-start(f32[4096]{0:T(1024)} %param.12) | copy-start | bytes 49156
  6.8 0.7 %copy-start.6 = (s32[2,32]{1,0:T(2,128)S(1)}, s32[2,32]{1,0:T(2,128)}, u32[]{:S(2)}) copy-start(s32[2,32]{1,0:T(2,128)} %gblocks_s.1) | copy-start | bytes 772
  7.5 0.7 %copy-start.7 = (s32[2,64]{1,0:T(2,128)S(1)}, s32[2,64]{1,0:T(2,128)}, u32[]{:S(2)}) copy-start(s32[2,64]{1,0:T(2,128)} %pairs_ref.1) | copy-start | bytes 1540
  8.1 0.7 %copy-start.8 = (f32[4]{0:T(128)S(1)}, f32[4]{0:T(128)}, u32[]{:S(2)}) copy-start(f32[4]{0:T(128)} %electro_ref.1) | copy-start | bytes 52
  8.8 0.7 %copy-start.9 = (f32[4]{0:T(128)S(1)}, f32[4]{0:T(128)}, u32[]{:S(2)}) copy-start(f32[4]{0:T(128)} %hard_ref.1) | copy-start | bytes 52

commit v2 on v1

--- a/solution.py
+++ b/solution.py
@@ -10,6 +10,7 @@
 TILE = 128
 ITERS = 3
 DIRECT = 16
+REACH = 0.9
 MESH = pl.DeviceIdType.MESH
 F32 = jnp.float32
 I32 = jnp.int32
@@ -54,19 +55,29 @@
 
 def kernel(
     sizes,
+    types_hbm,
+    potential_hbm,
+    guess_hbm,
+    electro_hbm,
+    hard_hbm,
+    local_hbm,
+    pairs_hbm,
+    count_hbm,
+    ghost_hbm,
+    gblocks_hbm,
+    send_hbm,
+    out_ref,
     types_ref,
     potential_ref,
     guess_ref,
     electro_ref,
     hard_ref,
-    local_hbm,
     pairs_ref,
     count_ref,
-    ghost_hbm,
     gblocks_ref,
     gblocks_s,
     send_ref,
-    out_ref,
+    small_sem,
     lt,
     gt,
     gp,
@@ -95,7 +106,7 @@
     part_sem,
     red_sem,
 ):
-    blocks = types_ref.shape[0]
+    blocks = types_hbm.shape[0]
     ahead, back, stages = places(sizes)
 
     barrier = pltpu.get_barrier_semaphore()
@@ -105,11 +116,31 @@
         for step in range(1, size):
             pl.semaphore_signal(barrier, inc=1, device_id=peer(step), device_id_type=MESH)
 
+    small = []
+    for at, (source, target) in enumerate(
+        (
+            (send_hbm, send_ref),
+            (guess_hbm, guess_ref),
+            (pairs_hbm, pairs_ref),
+            (count_hbm, count_ref),
+            (gblocks_hbm, gblocks_ref),
+            (gblocks_hbm, gblocks_s),
+            (types_hbm, types_ref),
+            (potential_hbm, potential_ref),
+            (electro_hbm, electro_ref),
+            (hard_hbm, hard_ref),
+        )
+    ):
+        copy = pltpu.make_async_copy(source, target, small_sem.at[at])
+        copy.start()
+        small.append(copy)
     load_local = pltpu.make_async_copy(local_hbm, lt, load_sem.at[0])
     load_local.start()
     load_ghost = pltpu.make_async_copy(ghost_hbm, gt, load_sem.at[1])
     load_ghost.start()
 
+    for copy in small:
+        copy.wait()
     for b in range(blocks):
         cut = slice(b * TILE, (b + 1) * TILE)
         piece = send_ref[:, cut]
@@ -117,7 +148,6 @@
         rows[1, b : b + 1, :] = piece[1:2]
         begin = guess_ref[:, cut]
         vec[0, b] = begin
-        xs[b] = begin
 
     slots = pairs_ref.shape[1]
     slot = lax.broadcasted_iota(I32, (blocks, slots), 1)
@@ -195,6 +225,16 @@
         electro = jnp.where(types == code, electro_ref[code], electro)
     wanted = -(electro + potential_ref[...])
     system = lax.broadcasted_iota(I32, (2, TILE), 0)
+    least = jnp.full((2, TILE), hard_ref[0], F32)
+    most = least
+    for code in range(1, hard_ref.shape[0]):
+        least = jnp.minimum(least, hard_ref[code])
+        most = jnp.maximum(most, hard_ref[code])
+    lowest = least - REACH
+    highest = most + REACH
+    middle = 0.5 * (least + most)
+    scale = 0.5 * (most - least + REACH)
+    shrink = 1.0 / scale
     for b in range(blocks):
         hd[b] = jnp.broadcast_to(hard[b : b + 1], (2, TILE))
         rs[b] = jnp.where(system == 0, jnp.broadcast_to(wanted[b : b + 1], (2, TILE)), -1.0)
@@ -341,62 +381,99 @@
         returned(apply)
         product = ps[...]
         if apply == 0:
-            residual = rs[...] - product
-            rs[...] = residual
-            vec[1] = residual
-            continue
-
-        residual = rs[...]
-        direction = vec[apply]
-        sums = jnp.concatenate(
-            [
-                jnp.sum(a * b, axis=0)
-                for a, b in (
-                    (residual, residual),
-                    (direction, product),
-                    (residual, product),
-                    (product, product),
-                )
-            ],
-            axis=0,
+            vec[1] = rs[...] - product
+        elif apply < ITERS:
+            vec[apply + 1] = (product - middle[None] * vec[apply]) * shrink[None]
+        else:
+            beyond = (product - middle[None] * vec[apply]) * shrink[None]
+
+    basis = [vec[apply] for apply in range(1, ITERS + 1)] + [beyond]
+    moments = 2 * ITERS
+    dots = [jnp.sum(basis[q // 2] * basis[(q + 1) // 2], axis=0) for q in range(moments)]
+    dots += [jnp.zeros((2, TILE), F32)] * (-moments % 4)
+    dots = jnp.concatenate(dots, axis=0)
+    sums = jnp.sum(dots, axis=1, keepdims=True)
+    lanes = lax.broadcasted_iota(I32, dots.shape, 1)
+    lines = lax.broadcasted_iota(I32, dots.shape, 0)
+    sums = jnp.sum(
+        jnp.where(lanes == lines, jnp.broadcast_to(sums, dots.shape), 0.0), axis=0, keepdims=True
+    )
+    offset = 0
+    sem_at = 0
+    for size, me, peer in stages:
+        mine = offset + me
+        red[mine] = sums
+        copies = []
+        for step in range(1, size):
+            copy = pltpu.make_async_remote_copy(
+                src_ref=red.at[mine],
+                dst_ref=red.at[mine],
+                send_sem=red_sem.at[0, sem_at],
+                recv_sem=red_sem.at[1, sem_at],
+                device_id=peer(step),
+                device_id_type=MESH,
+            )
+            copy.start()
+            copies.append(copy)
+            sem_at += 1
+        for copy in copies:
+            copy.wait()
+        sums = jnp.sum(red[offset : offset + size], axis=0)
+        offset += size
+    spot = lax.broadcasted_iota(I32, (2, TILE), 1) - system
+    moment = [
+        jnp.broadcast_to(
+            jnp.sum(
+                jnp.where(spot == 2 * q, jnp.broadcast_to(sums, (2, TILE)), 0.0),
+                axis=1,
+                keepdims=True,
+            ),
+            (2, TILE),
         )
-        offset = 0
-        sem_at = 0
-        for size, me, peer in stages:
-            mine = offset + me
-            red[apply - 1, mine] = sums
-            copies = []
-            for step in range(1, size):
-                copy = pltpu.make_async_remote_copy(
-                    src_ref=red.at[apply - 1, mine],
-                    dst_ref=red.at[apply - 1, mine],
-                    send_sem=red_sem.at[0, apply - 1, sem_at],
-                    recv_sem=red_sem.at[1, apply - 1, sem_at],
-                    device_id=peer(step),
-                    device_id_type=MESH,
-                )
-                copy.start()
-                copies.append(copy)
-                sem_at += 1
-            for copy in copies:
-                copy.wait()
-            sums = jnp.sum(red[apply - 1, offset : offset + size], axis=0)
-            offset += size
-        totals = jnp.broadcast_to(jnp.sum(sums, axis=1, keepdims=True), (8, TILE))
-        norm_now = totals[0:2]
-        step_size = norm_now / totals[2:4]
-        found = xs[...] + step_size[None] * direction
-        if apply == ITERS:
-            xs[...] = found
-        else:
-            xs[...] = found
-            ratio = jnp.maximum(
-                (norm_now + step_size * (step_size * totals[6:8] - 2.0 * totals[4:6])) / norm_now,
-                0.0,
-            )
-            residual = residual - step_size[None] * product
-            rs[...] = residual
-            vec[apply + 1] = residual + ratio[None] * direction
+        for q in range(moments)
+    ]
+
+    def product_of(a, b):
+        total = None
+        for p, a_p in enumerate(a):
+            for q, b_q in enumerate(b):
+                term = a_p * b_q * moment[p + q]
+                total = term if total is None else total + term
+        return total
+
+    def add(a, b, factor):
+        longer = max(len(a), len(b))
+        out = []
+        for q in range(longer):
+            if q >= len(a):
+                out.append(factor * b[q])
+            elif q >= len(b):
+                out.append(a[q])
+            else:
+                out.append(a[q] + factor * b[q])
+        return out
+
+    one = jnp.ones((2, TILE), F32)
+    residual = [one]
+    direction = [one]
+    solved = []
+    norm_now = moment[0]
+    for iteration in range(ITERS):
+        image = [middle * q for q in direction]
+        image = add(image, [0.0 * one] + direction, scale)
+        step_size = norm_now / product_of(direction, image)
+        step_size = jnp.minimum(jnp.maximum(step_size, 1.0 / highest), 1.0 / lowest)
+        solved = add(solved, direction, step_size)
+        if iteration + 1 < ITERS:
+            residual = add(residual, image, -step_size)
+            norm_next = jnp.maximum(product_of(residual, residual), 1e-20 * moment[0])
+            ratio = jnp.minimum(norm_next / norm_now, highest / lowest)
+            direction = add(residual, direction, ratio)
+            norm_now = norm_next
+    found = vec[0]
+    for factor, vector in zip(solved, basis):
+        found = found + factor[None] * vector
+    xs[...] = found
 
     for b in range(blocks):
         out_ref[:, b * TILE : (b + 1) * TILE] = xs[b]
@@ -424,17 +501,27 @@
     else:
         places_held, peers = n_gx + n_gy * n_gz, n_gx + n_gy * n_gz - 2
     vmem = pl.BlockSpec(memory_space=pltpu.VMEM)
-    smem = pl.BlockSpec(memory_space=pltpu.SMEM)
-    hbm = pl.BlockSpec(memory_space=pl.ANY)
+    hbm = pl.BlockSpec(memory_space=pltpu.HBM)
     applies = ITERS + 1
     vector = (blocks, 2, TILE)
     dma = pltpu.SemaphoreType.DMA
     call = pl.pallas_call(
         functools.partial(kernel, sizes),
         out_shape=jax.ShapeDtypeStruct(guess.shape, F32),
-        in_specs=[vmem, vmem, vmem, smem, smem, hbm, vmem, smem, hbm, vmem, smem, vmem],
+        in_specs=[hbm] * 11,
         out_specs=vmem,
         scratch_shapes=[
+            pltpu.VMEM((blocks, TILE), I32),
+            pltpu.VMEM((blocks, TILE), F32),
+            pltpu.VMEM(guess.shape, F32),
+            pltpu.SMEM(type_electroneg.shape, F32),
+            pltpu.SMEM(type_hardness.shape, F32),
+            pltpu.VMEM(local_pairs.shape, I32),
+            pltpu.SMEM(local_count.shape, I32),
+            pltpu.VMEM(ghost_blocks.shape, I32),
+            pltpu.SMEM(ghost_blocks.shape, I32),
+            pltpu.VMEM(send_rows.shape, I32),
+            dma((10,)),
             pltpu.VMEM((slots, TILE, TILE), jnp.bfloat16),
             pltpu.VMEM((2, blocks, TILE, TILE), jnp.bfloat16),
             pltpu.VMEM((2, blocks, TILE, TILE), jnp.bfloat16),
@@ -456,15 +543,15 @@
             pltpu.VMEM(vector, F32),
             pltpu.VMEM(vector, F32),
             pltpu.VMEM(vector, F32),
-            pltpu.VMEM((ITERS, places_held, 8, TILE), F32),
+            pltpu.VMEM((places_held, 1, TILE), F32),
             dma((5,)),
             dma((2, 2)),
             dma((2, applies, 2)),
             dma((2, applies, 2)),
-            dma((2, ITERS, peers)),
+            dma((2, peers)),
         ],
         compiler_params=pltpu.CompilerParams(
-            collective_id=0, has_side_effects=True, vmem_limit_bytes=40 * 1024 * 1024
+            collective_id=0, has_side_effects=True, vmem_limit_bytes=60 * 1024 * 1024
         ),
         name="charges",
     )
@@ -478,7 +565,6 @@
         local_pairs,
         local_count,
         ghost_tiles,
-        ghost_blocks,
         ghost_blocks,
         send_rows,
     )

time: 58.1 us -> 40.6 us (0.70)
  Pallas kernels: 47.5 us -> 38.4 us
  local copies, waits for them, and re-layouts: 9.41 us -> 1.38 us
    pallas_call x1, Pallas kernels: 47.5 us -> 38.4 us  [shards(): call(atom_types.reshape(blocks, TILE), potential.reshape(blocks, TILE), g...]
    unnamed x21 -> x1, local copies, waits for them, and re-layouts: 9.41 us -> 1.38 us
where the time goes in v2:
time: 40.6 us; the launch traced here: 40.4 us
  Pallas kernels  38.4 us (95%)
  local copies, waits for them, and re-layouts  1.38 us (3%)
  between operations  0.66 us (2%)
    pallas_call x1, Pallas kernels, shards(): call(atom_types.reshape(blocks, TILE), potential.reshape(blocks, TILE), g...  38.4 us
    unnamed x1, local copies, waits for them, and re-layouts  1.38 us

profile of v2, /device:TPU:0, one launch (start us, length us, event | category | flops | bytes accessed | tf_op | source)
XLA Modules:
  0.0 40.4 jit_solution(10574192841739480313)
XLA Ops:
  0.7 38.4 %charges.1 = f32[2,4096]{1,0:T(2,128)} custom-call(s32[32,128]{1,0:T(8,128)} %bitcast.2, f32[32,128]{1,0:T(8,128)} %bitcast.3, f32[2,4096]{1,0:T(2,128)} %guess_hbm.1, f32[4]{0:T(128)} %electro_hbm.1, f32[4]{0:T(128)} %hard_hbm.1, bf16[64,128,128]{2,1,0:T(8,128)(2,1)} %local_hbm.1, s32[2,64]{1,0:T(2,128)} %pairs_hbm.1, s32[1]{0:T(128)S(6)} %copy.13.count_hbm, ...), custom_call_target="tpu_custom_call" | custom-call | tf_op jit(solution)/shard_map/charges/pallas_call | solution.py:558
  39.1 1.4 %copy.14 = f32[2,4096]{1,0:T(2,128)} copy(f32[2,4096]{1,0:T(2,128)} %charges.1) | data formatting | bytes 65536

commit v3 on v2

--- a/solution.py
+++ b/solution.py
@@ -1,4 +1,5 @@
 import functools
+import math
 
 import jax
 import jax.numpy as jnp
@@ -139,7 +140,7 @@
     load_ghost = pltpu.make_async_copy(ghost_hbm, gt, load_sem.at[1])
     load_ghost.start()
 
-    for copy in small:
+    for copy in small[:2]:
         copy.wait()
     for b in range(blocks):
         cut = slice(b * TILE, (b + 1) * TILE)
@@ -149,6 +150,37 @@
         begin = guess_ref[:, cut]
         vec[0, b] = begin
 
+    pl.semaphore_wait(barrier, greeted)
+
+    rows_copy = []
+    for d in range(2):
+        copy = pltpu.make_async_remote_copy(
+            src_ref=rows.at[d],
+            dst_ref=rows_in.at[d],
+            send_sem=rows_sem.at[0, d],
+            recv_sem=rows_sem.at[1, d],
+            device_id=back[d],
+            device_id_type=MESH,
+        )
+        copy.start()
+        rows_copy.append(copy)
+
+    def send(buffer, landing, sems, apply, d, target):
+        copy = pltpu.make_async_remote_copy(
+            src_ref=buffer,
+            dst_ref=landing,
+            send_sem=sems.at[0, apply, d],
+            recv_sem=sems.at[1, apply, d],
+            device_id=target,
+            device_id_type=MESH,
+        )
+        copy.start()
+        return copy
+
+    first_sends = [send(vec.at[0], vec_in.at[0, d], vec_sem, 0, d, back[d]) for d in range(2)]
+
+    for copy in small[2:]:
+        copy.wait()
     slots = pairs_ref.shape[1]
     slot = lax.broadcasted_iota(I32, (blocks, slots), 1)
     block = lax.broadcasted_iota(I32, (blocks, slots), 0)
@@ -190,33 +222,6 @@
     load_own = pltpu.make_async_copy(own_v, own_s, load_sem.at[3])
     load_own.start()
 
-    pl.semaphore_wait(barrier, greeted)
-
-    rows_copy = []
-    for d in range(2):
-        copy = pltpu.make_async_remote_copy(
-            src_ref=rows.at[d],
-            dst_ref=rows_in.at[d],
-            send_sem=rows_sem.at[0, d],
-            recv_sem=rows_sem.at[1, d],
-            device_id=back[d],
-            device_id_type=MESH,
-        )
-        copy.start()
-        rows_copy.append(copy)
-
-    def send(buffer, landing, sems, apply, d, target):
-        copy = pltpu.make_async_remote_copy(
-            src_ref=buffer,
-            dst_ref=landing,
-            send_sem=sems.at[0, apply, d],
-            recv_sem=sems.at[1, apply, d],
-            device_id=target,
-            device_id_type=MESH,
-        )
-        copy.start()
-        return copy
-
     types = types_ref[...]
     hard = jnp.zeros(types.shape, F32)
     electro = jnp.zeros(types.shape, F32)
@@ -260,6 +265,8 @@
         )
 
     def looped(steps, unroll, body):
+        unroll = math.gcd(steps, unroll)
+
         def run(outer, carry):
             for inner in range(unroll):
                 body(outer * unroll + inner)
@@ -267,7 +274,7 @@
 
         lax.fori_loop(0, steps // unroll, run, 0)
 
-    def local_part(apply):
+    def local_part(apply, last=False):
         def body(pair):
             one = pair * 2
             two = one + 1
@@ -278,6 +285,11 @@
             onward = dot(
                 left, square(lt[s[0][0]], lt[s[1][0]], lt[s[0][1]], lt[s[1][1]]), NT
             )
+            if last:
+                sum_one, sum_two = parts_of(onward)
+                ps[one] = hd[one] * vec[apply, one] + 2.0 * sum_one
+                ps[two] = hd[two] * vec[apply, two] + 2.0 * sum_two
+                return
             left = jnp.concatenate(
                 [join(lh[s[6][0]], lh[s[6][1]]), join(lh[s[7][0]], lh[s[7][1]])], axis=1
             )
@@ -288,7 +300,7 @@
             ps[one] = hd[one] * vec[apply, one] + sum_one
             ps[two] = hd[two] * vec[apply, two] + sum_two
 
-        looped(blocks // 2, 4, body)
+        looped(blocks // 2, 16, body)
 
     def partials(apply):
         def body(k):
@@ -298,9 +310,9 @@
             part[apply, 0, k] = zero
             part[apply, 1, k] = first
 
-        looped(blocks, 8, body)
-
-    def ghost_part():
+        looped(blocks, 32, body)
+
+    def ghost_part(last):
         def body(pair):
             one = pair * 2
             two = one + 1
@@ -316,16 +328,18 @@
             sum_one, sum_two = parts_of(
                 dot(left, square(gp[0, k0[0]], gp[1, k1[0]], gp[0, k0[1]], gp[1, k1[1]]), NT)
             )
+            if last:
+                sum_one, sum_two = 2.0 * sum_one, 2.0 * sum_two
             ps[one] = ps[one] + sum_one
             ps[two] = ps[two] + sum_two
 
-        looped(blocks // 2, 4, body)
+        looped(blocks // 2, 16, body)
 
     def returned(apply):
         def body(b):
             ps[b] = ps[b] + (part_in[apply][0][own_s[0, b]] + part_in[apply][1][own_s[1, b]])
 
-        looped(blocks, 8, body)
+        looped(blocks, 32, body)
 
     def reorder():
         within_at = lax.broadcasted_iota(I32, (TILE, TILE), 0)
@@ -338,15 +352,17 @@
                 chosen = jnp.where(within == within_at, 1.0, 0.0).astype(jnp.bfloat16)
                 gp[d, k] = dot(gt[d, k], chosen, NT).astype(jnp.bfloat16)
 
-            looped(blocks, 4, body)
-
-    pending = []
+            looped(blocks, 16, body)
+
     for apply in range(ITERS + 1):
-        incoming = []
-        for d in range(2):
-            incoming.append(
+        last = apply == ITERS
+        if apply == 0:
+            incoming = first_sends
+        else:
+            incoming = [
                 send(vec.at[apply], vec_in.at[apply, d], vec_sem, apply, d, back[d])
-            )
+                for d in range(2)
+            ]
         lh[0:blocks] = split(vec[apply])
         if apply == 0:
             load_local.wait()
@@ -364,21 +380,23 @@
             reorder()
             load_next.wait()
             load_own.wait()
-        partials(apply)
         back_copies = []
-        for d in range(2):
-            back_copies.append(
-                send(part.at[apply, d], part_in[apply][d], part_sem, apply, d, ahead[d])
-            )
+        if not last:
+            partials(apply)
+            for d in range(2):
+                back_copies.append(
+                    send(part.at[apply, d], part_in[apply][d], part_sem, apply, d, ahead[d])
+                )
         if apply > 0:
-            local_part(apply)
+            local_part(apply, last)
         for d in range(2):
             incoming[d].wait()
             gl[d] = split(vec_in[apply, d])
-        ghost_part()
+        ghost_part(last)
         for copy in back_copies:
             copy.wait()
-        returned(apply)
+        if not last:
+            returned(apply)
         product = ps[...]
         if apply == 0:
             vec[1] = rs[...] - product

time: 40.6 us -> 37.1 us (0.914)
  Pallas kernels: 38.4 us -> 34.9 us
    pallas_call x1, Pallas kernels: 38.4 us -> 34.9 us  [shards(): call(atom_types.reshape(blocks, TILE), potential.reshape(blocks, TILE), g...]
where the time goes in v3:
time: 37.1 us; the launch traced here: 36.9 us
  Pallas kernels  34.9 us (94%)
  local copies, waits for them, and re-layouts  1.38 us (4%)
  between operations  0.66 us (2%)
    pallas_call x1, Pallas kernels, shards(): call(atom_types.reshape(blocks, TILE), potential.reshape(blocks, TILE), g...  34.9 us
    unnamed x1, local copies, waits for them, and re-layouts  1.38 us

profile of v3, /device:TPU:0, one launch (start us, length us, event | category | flops | bytes accessed | tf_op | source)
XLA Modules:
  0.0 36.9 jit_solution(4722489320609199436)
XLA Ops:
  0.7 34.9 %charges.1 = f32[2,4096]{1,0:T(2,128)} custom-call(s32[32,128]{1,0:T(8,128)} %bitcast.2, f32[32,128]{1,0:T(8,128)} %bitcast.3, f32[2,4096]{1,0:T(2,128)} %guess_hbm.1, f32[4]{0:T(128)} %electro_hbm.1, f32[4]{0:T(128)} %hard_hbm.1, bf16[64,128,128]{2,1,0:T(8,128)(2,1)} %local_hbm.1, s32[2,64]{1,0:T(2,128)} %pairs_hbm.1, s32[1]{0:T(128)S(6)} %copy.13.count_hbm, ...), custom_call_target="tpu_custom_call" | custom-call | tf_op jit(solution)/shard_map/charges/pallas_call | solution.py:576
  35.5 1.4 %copy.14 = f32[2,4096]{1,0:T(2,128)} copy(f32[2,4096]{1,0:T(2,128)} %charges.1) | data formatting | bytes 65536

commit v4 on v3

--- a/solution.py
+++ b/solution.py
@@ -389,6 +389,11 @@
                 )
         if apply > 0:
             local_part(apply, last)
+        if last:
+            early = [
+                jnp.sum(vec[1 + q // 2] * vec[1 + (q + 1) // 2], axis=0)
+                for q in range(2 * ITERS - 1)
+            ]
         for d in range(2):
             incoming[d].wait()
             gl[d] = split(vec_in[apply, d])
@@ -407,7 +412,7 @@
 
     basis = [vec[apply] for apply in range(1, ITERS + 1)] + [beyond]
     moments = 2 * ITERS
-    dots = [jnp.sum(basis[q // 2] * basis[(q + 1) // 2], axis=0) for q in range(moments)]
+    dots = early + [jnp.sum(basis[ITERS - 1] * beyond, axis=0)]
     dots += [jnp.zeros((2, TILE), F32)] * (-moments % 4)
     dots = jnp.concatenate(dots, axis=0)
     sums = jnp.sum(dots, axis=1, keepdims=True)

time: 37.1 us -> 37.1 us (level)
  no operation moved by 1% of the time
where the time goes in v4:
time: 37.1 us; the launch traced here: 36.9 us
  Pallas kernels  34.9 us (94%)
  local copies, waits for them, and re-layouts  1.38 us (4%)
  between operations  0.66 us (2%)
    pallas_call x1, Pallas kernels, shards(): call(atom_types.reshape(blocks, TILE), potential.reshape(blocks, TILE), g...  34.9 us
    unnamed x1, local copies, waits for them, and re-layouts  1.38 us

profile of v4, /device:TPU:0, one launch (start us, length us, event | category | flops | bytes accessed | tf_op | source)
XLA Modules:
  0.0 36.9 jit_solution(5342522270232873825)
XLA Ops:
  0.7 34.9 %charges.1 = f32[2,4096]{1,0:T(2,128)} custom-call(s32[32,128]{1,0:T(8,128)} %bitcast.2, f32[32,128]{1,0:T(8,128)} %bitcast.3, f32[2,4096]{1,0:T(2,128)} %guess_hbm.1, f32[4]{0:T(128)} %electro_hbm.1, f32[4]{0:T(128)} %hard_hbm.1, bf16[64,128,128]{2,1,0:T(8,128)(2,1)} %local_hbm.1, s32[2,64]{1,0:T(2,128)} %pairs_hbm.1, s32[1]{0:T(128)S(6)} %copy.13.count_hbm, ...), custom_call_target="tpu_custom_call" | custom-call | tf_op jit(solution)/shard_map/charges/pallas_call | solution.py:581
  35.5 1.4 %copy.14 = f32[2,4096]{1,0:T(2,128)} copy(f32[2,4096]{1,0:T(2,128)} %charges.1) | data formatting | bytes 65536
